TPU v7x, 32 devices: a whole 2x2x4 slice. The times are simulated.
32 devices in a mesh: dp: 4 (over x, core), fsdp: 4 (over z), tensor: 2 (over y).
Axes of the slice: x: 2, y: 2, z: 4, core: 2. Of those that a mesh axis runs over, the one named last changes fastest.
Arguments:
- activations: bfloat16 [4096, 4096], P(('dp', 'tensor'), 'fsdp'), may hold values from -6 to 6
- cotangent: bfloat16 [4096, 16384], P('dp', 'tensor'), may hold values from -6 to 6
- weight: bfloat16 [4096, 16384], P('fsdp', 'tensor'), may hold values from -0.046875 to 0.046875
- residual: bfloat16 [4, 4096, 16384], P('dp', 'fsdp', 'tensor'), may hold values from -6 to 6
- step_size: float32 [1], replicated, may hold values from 0.02 to 0.06
- kept_blocks: int32 [4, 4, 2, 8], P('dp', 'fsdp', 'tensor'), may hold values from 0 to 511, as said below
Outputs:
- input_grad: bfloat16 [4096, 4096], P(('dp', 'tensor'), 'fsdp')
- residual_out: bfloat16 [4, 4096, 16384], P('dp', 'fsdp', 'tensor')
- owned: float32 [4, 4, 2, 128, 128, 128], P('dp', 'fsdp', 'tensor')
Inputs may be any that keep to these rules, and one draw needn't show every extreme that they name: The 8 entries of kept_blocks[a, f, t, :] are different block numbers.
All inputs are finite; a program needn't handle non-finite values.
Results may differ from a plain program's by a relative error of at most 0.0029.
Values may be sent and summed in bfloat16 or wider, within the bound.
No kernel may reach another device: no remote copies, remote signals or barrier semaphores. Data moves between devices by JAX's collectives and lax.ppermute only.
A program may use at most 128 MiB of HBM per device.

v0:
```python
import functools

import jax
import jax.numpy as jnp
from jax import lax
from jax.experimental import pallas as pl
from jax.experimental.pallas import tpu as pltpu
from jax.sharding import PartitionSpec as P

BLK = 128
MIB = 1024 * 1024
LABEL_ROWS = 16
RADIX = 16


def cost(flops, nbytes):
    return pl.CostEstimate(flops=flops, bytes_accessed=nbytes, transcendentals=0)


def params(mib=62):
    return pltpu.CompilerParams(vmem_limit_bytes=mib * MIB)


def dot_nt(a, b):
    return lax.dot_general(a, b, (((1,), (1,)), ((), ())), preferred_element_type=jnp.float32)


def dot_nn(a, b):
    return lax.dot_general(a, b, (((1,), (0,)), ((), ())), preferred_element_type=jnp.float32)


def hidden_chunks(cols):
    sizes = []
    for size in (512, 1536, 2048, 4096):
        if cols > sum(sizes):
            sizes.append(min(size, cols - sum(sizes)))
    while sum(sizes) < cols:
        sizes.append(min(4096, cols - sum(sizes)))
    return sizes


def smem():
    return pl.BlockSpec(memory_space=pltpu.SMEM)


def vmem():
    return pl.BlockSpec(memory_space=pltpu.VMEM)


def hbm():
    return pl.BlockSpec(memory_space=pltpu.HBM)


def in_hbm(x):
    return pltpu.with_memory_space_constraint(x, pltpu.HBM)


def in_vmem(x):
    return pltpu.with_memory_space_constraint(x, pltpu.VMEM)


def cot_copies(here_ref, split, cot_ref, buf_ref, sems):
    if not split:
        return [pltpu.make_async_copy(cot_ref, buf_ref, sems.at[0])]
    half = buf_ref.shape[0] // 2
    copies = []
    for i, at in enumerate((here_ref[0], 1 - here_ref[0])):
        rows = pl.ds(pl.multiple_of(at * half, half), half)
        copies.append(pltpu.make_async_copy(cot_ref.at[rows], buf_ref.at[pl.ds(i * half, half)], sems.at[i]))
    return copies


def input_grad_kernel(split, sizes, zero_copies, here_ref, kept_ref, cot_ref, w_ref, res_ref, *refs):
    if split:
        acts_ref, away_ref, acts_t_ref, *refs = refs
    own_ref, owned_ref, kept_cot_ref, kept_res_ref, *refs = refs
    acc_ref, cot_buf, w_buf, zero_ref, cot_sem, w_sem, zero_sem, kept_cot_sem, kept_res_sem, *refs = refs
    zero_rows = zero_ref.shape[0]
    rows, hidden = w_ref.shape
    width = min(256, rows)
    last = len(sizes) - 1
    keep = kept_cot_ref.shape[0]
    half = own_ref.shape[0]

    def loads(i):
        part = pl.ds(sum(sizes[:i]), sizes[i])
        return cot_copies(here_ref, split, cot_ref.at[:, part], cot_buf.at[:, part], cot_sem.at[i]) + [
            pltpu.make_async_copy(w_ref.at[:, part], w_buf.at[:, part], w_sem.at[i])
        ]

    def start(i):
        if i <= last:
            for copy in loads(i):
                copy.start()

    def zero_copy(i):
        return pltpu.make_async_copy(zero_ref, owned_ref.at[pl.ds(i * zero_rows, zero_rows)], zero_sem.at[i])

    def kept_copies(k):
        col_blocks = hidden // BLK
        row = pl.ds(pl.multiple_of(kept_ref[k] // col_blocks * BLK, BLK), BLK)
        col = pl.ds(pl.multiple_of(kept_ref[k] % col_blocks * BLK, BLK), BLK)
        return (
            pltpu.make_async_copy(cot_buf.at[:, col], kept_cot_ref.at[k], kept_cot_sem.at[k]),
            pltpu.make_async_copy(res_ref.at[row, col], kept_res_ref.at[k], kept_res_sem.at[k]),
        )

    if split:
        acts_buf, acts_sem = refs
        acts_copy = pltpu.make_async_copy(acts_ref, acts_buf, acts_sem)
        acts_copy.start()
    start(0)
    if split:
        acts_copy.wait()
        acts_t_ref[:, :half] = acts_buf[...].T
    start(1)
    zero_ref[...] = jnp.zeros_like(zero_ref)
    for i in range(last + 1):
        for copy in loads(i):
            copy.wait()
        start(i + 2)
        if i == last:
            for z in range(zero_copies):
                zero_copy(z).start()
            for k in range(keep):
                for copy in kept_copies(k):
                    copy.start()
        part = slice(sum(sizes[:i]), sum(sizes[: i + 1]))
        for at in range(0, rows, width):
            cols = slice(at, at + width)
            total = dot_nt(cot_buf[:, part], w_buf[cols, part])
            if i > 0:
                total += acc_ref[:, cols]
            if i < last:
                acc_ref[:, cols] = total
            else:
                own_ref[:, cols] = total[:half]
                if split:
                    away_ref[:, cols] = total[half:].astype(jnp.bfloat16)
    for z in range(zero_copies):
        zero_copy(z).wait()
    for k in range(keep):
        for copy in kept_copies(k):
            copy.wait()


def input_grad_partials(here, kept, cot, weight, residual, owned_count, acts):
    split = acts is not None
    tokens, cols = cot.shape
    rows = weight.shape[0]
    sizes = hidden_chunks(cols)
    keep = kept.shape[0]
    own_rows = tokens // 2 if split else tokens
    zero_rows = min(16, owned_count)
    zero_copies = owned_count // zero_rows
    out_shape = [
        pltpu.VMEM((own_rows, rows), jnp.float32) if split else jax.ShapeDtypeStruct((own_rows, rows), jnp.float32),
        pltpu.HBM((owned_count, BLK, BLK), jnp.float32),
        pltpu.VMEM((keep, tokens, BLK), jnp.bfloat16),
        pltpu.VMEM((keep, BLK, BLK), jnp.bfloat16),
    ]
    out_specs = [vmem(), hbm(), vmem(), vmem()]
    scratch = [
        pltpu.VMEM((tokens, rows), jnp.float32),
        pltpu.VMEM((tokens, cols), jnp.bfloat16),
        pltpu.VMEM((rows, cols), jnp.bfloat16),
        pltpu.VMEM((zero_rows, BLK, BLK), jnp.float32),
        pltpu.SemaphoreType.DMA((len(sizes), 2)),
        pltpu.SemaphoreType.DMA((len(sizes),)),
        pltpu.SemaphoreType.DMA((zero_copies,)),
        pltpu.SemaphoreType.DMA((keep,)),
        pltpu.SemaphoreType.DMA((keep,)),
    ]
    if split:
        out_shape = [
            jax.ShapeDtypeStruct((own_rows, rows), jnp.bfloat16),
            pltpu.VMEM((rows, tokens), jnp.bfloat16),
        ] + out_shape
        out_specs = [vmem(), vmem()] + out_specs
        scratch += [pltpu.VMEM(acts.shape, jnp.bfloat16), pltpu.SemaphoreType.DMA]
    return pl.pallas_call(
        functools.partial(input_grad_kernel, split, sizes, zero_copies),
        out_shape=out_shape,
        in_specs=[smem(), smem()] + [hbm()] * (3 + split),
        out_specs=out_specs,
        scratch_shapes=scratch,
        compiler_params=params(52),
        cost_estimate=cost(2 * tokens * rows * cols, 2 * cols * (tokens + rows) + 4 * owned_count * BLK * BLK),
        name="input_grad_partials",
    )(here, kept, in_hbm(cot), in_hbm(weight), in_hbm(residual), *([in_hbm(acts)] if split else []))


def kept_kernel(pair, col_blocks, kept_ref, step_ref, *refs):
    if pair:
        _, *refs = refs
    act_ref, cot_ref, res_ref, acts_t_ref, out_ref = refs
    keep = cot_ref.shape[0]
    acts_t_ref[:, acts_t_ref.shape[1] - act_ref.shape[0] :] = act_ref[...].T
    for k in range(keep):
        row = pl.ds(pl.multiple_of(kept_ref[k] // col_blocks * BLK, BLK), BLK)
        gradient = dot_nn(acts_t_ref[row, :], cot_ref[k])
        out_ref[k * BLK : (k + 1) * BLK, :] = (res_ref[k].astype(jnp.float32) + step_ref[0] * gradient).astype(
            jnp.bfloat16
        )
    lane = lax.broadcasted_iota(jnp.int32, (LABEL_ROWS, BLK), 1) % keep
    low = lax.broadcasted_iota(jnp.int32, (LABEL_ROWS, BLK), 0) % 2 == 1
    label = jnp.zeros((LABEL_ROWS, BLK), jnp.int32)
    for k in range(keep):
        digit = jnp.where(low, kept_ref[k] % RADIX, kept_ref[k] // RADIX)
        label = jnp.where(lane == k, digit, label)
    out_ref[keep * BLK :, :] = label.astype(jnp.float32).astype(jnp.bfloat16)


def kept_blocks_of(kept, step_size, acts_t, act, kept_cot, kept_res, col_blocks):
    rows = act.shape[1]
    keep, tokens = kept_cot.shape[:2]
    pair = acts_t is not None
    return pl.pallas_call(
        functools.partial(kept_kernel, pair, col_blocks),
        out_shape=[
            pltpu.VMEM((rows, tokens), jnp.bfloat16),
            jax.ShapeDtypeStruct((keep * BLK + LABEL_ROWS, BLK), jnp.bfloat16),
        ],
        in_specs=[smem()] * 2 + [vmem()] * (3 + pair),
        out_specs=[vmem(), vmem()],
        input_output_aliases={2: 0} if pair else {},
        compiler_params=params(16),
        cost_estimate=cost(2 * tokens * BLK * BLK * keep, 4 * tokens * rows + 2 * keep * tokens * BLK),
        name="kept_blocks",
    )(kept, step_size, *([in_vmem(acts_t)] if pair else []), act, in_vmem(kept_cot), in_vmem(kept_res))


def residual_kernel(split, here_ref, step_ref, acts_t_ref, cot_ref, res_ref, out_ref, cot_buf, res_buf, *sems):
    cot_sem, res_sem, out_sem = sems
    step = step_ref[0]
    chunks, _, chunk = cot_buf.shape
    width = min(256, chunk)

    def columns(j):
        return pl.ds(pl.multiple_of(j * chunk, chunk), chunk)

    def loads(j):
        return cot_copies(here_ref, split, cot_ref.at[:, columns(j)], cot_buf.at[j], cot_sem.at[j]) + [
            pltpu.make_async_copy(res_ref.at[:, columns(j)], res_buf.at[j], res_sem.at[j])
        ]

    def store(j):
        return pltpu.make_async_copy(res_buf.at[j], out_ref.at[:, columns(j)], out_sem.at[j])

    def start(j):
        @pl.when(j < chunks)
        def _():
            for copy in loads(j):
                copy.start()

    start(0)
    start(1)

    @pl.loop(0, chunks)
    def _(j):
        for copy in loads(j):
            copy.wait()
        start(j + 2)
        for at in range(0, chunk, width):
            part = slice(at, at + width)
            gradient = dot_nn(acts_t_ref[...], cot_buf[j, :, part])
            res_buf[j, :, part] = (res_buf[j, :, part].astype(jnp.float32) + step * gradient).astype(jnp.bfloat16)
        store(j).start()

    for j in range(chunks):
        store(j).wait()


def residual_of(here, step_size, acts_t, cot, residual, split):
    tokens, cols = cot.shape
    rows = residual.shape[0]
    chunk = min(1024, cols)
    chunks = cols // chunk
    sem = pltpu.SemaphoreType.DMA((chunks,))
    return pl.pallas_call(
        functools.partial(residual_kernel, split),
        out_shape=pltpu.HBM((rows, cols), jnp.bfloat16),
        in_specs=[smem()] * 2 + [vmem(), hbm(), hbm()],
        out_specs=hbm(),
        scratch_shapes=[
            pltpu.VMEM((chunks, tokens, chunk), jnp.bfloat16),
            pltpu.VMEM((chunks, rows, chunk), jnp.bfloat16),
            pltpu.SemaphoreType.DMA((chunks, 2)),
            sem,
            sem,
        ],
        compiler_params=params(44),
        cost_estimate=cost(2 * tokens * rows * cols, 2 * tokens * (rows + cols) + 4 * rows * cols),
        name="residual_out",
    )(here, step_size, in_vmem(acts_t), in_hbm(cot), in_hbm(residual))


def finish_kernel(groups, keep, pair, col_blocks, me_ref, kept_ref, *refs):
    if pair:
        own_ref, arrived_ref, *refs = refs
    block_refs = refs[:groups]
    refs = refs[groups + 2 :]
    if pair:
        grad_ref, *refs = refs
    out_ref, res_ref, sum_ref, table_ref, scalar_ref, zero_ref, sem, table_sem, zero_sem, *refs = refs
    total = groups * keep
    me = me_ref[0]

    zero_ref[...] = jnp.zeros_like(zero_ref)
    zero_copies = []
    for k in range(keep):
        at = pl.multiple_of(kept_ref[k] // col_blocks * BLK, BLK)
        col = pl.multiple_of(kept_ref[k] % col_blocks * BLK, BLK)
        zero_copies.append(
            pltpu.make_async_copy(zero_ref, res_ref.at[pl.ds(at, BLK), pl.ds(col, BLK)], zero_sem.at[k])
        )
        zero_copies[k].start()

    row = lax.broadcasted_iota(jnp.int32, (total, BLK), 0)
    lane = lax.broadcasted_iota(jnp.int32, (total, BLK), 1)
    numbers = jnp.full((total, BLK), -1, jnp.int32)
    for g, block_ref in enumerate(block_refs):
        digits = block_ref[keep * BLK :, :].astype(jnp.float32).astype(jnp.int32)
        numbers = jnp.where(lane // keep == g, digits[0:1, :] * RADIX + digits[1:2, :], numbers)
    numbers = numbers.astype(jnp.float32)
    number = jnp.sum(jnp.where(lane == row, numbers, 0.0), axis=1, keepdims=True)
    first = jnp.min(jnp.where(numbers == number, lane.astype(jnp.float32), float(BLK)), axis=1, keepdims=True)
    number = jnp.broadcast_to(number, (total, BLK)).astype(jnp.int32)
    first = jnp.broadcast_to(first, (total, BLK)).astype(jnp.int32)
    table_ref[...] = jnp.where(lane == 0, jnp.where(number % groups == me, first, -1), number // groups)
    table = pltpu.make_async_copy(table_ref, scalar_ref, table_sem)
    table.start()

    grad_copies = []
    if pair:
        grad_buf, grad_sem = refs
        size = grad_buf.shape[0] // grad_sem.shape[0]
        for c in range(grad_sem.shape[0]):
            part = slice(c * size, (c + 1) * size)
            grad_buf[part, :] = (own_ref[part, :] + arrived_ref[part, :].astype(jnp.float32)).astype(jnp.bfloat16)
            grad_copies.append(pltpu.make_async_copy(grad_buf.at[part, :], grad_ref.at[part, :], grad_sem.at[c]))
            grad_copies[c].start()

    table.wait()

    def copy(i):
        return pltpu.make_async_copy(sum_ref.at[i], out_ref.at[scalar_ref[i, 1]], sem.at[i])

    def block(i):
        at = i % keep * BLK
        return block_refs[i // keep][at : at + BLK, :].astype(jnp.float32)

    for i in range(total):
        slot = scalar_ref[i, 0]

        @pl.when(slot == i)
        def _(i=i):
            sum_ref[i] = block(i)

        if i >= keep:

            @pl.when((slot >= 0) & (slot < i))
            def _(i=i, slot=slot):
                sum_ref[slot] += block(i)

    for i in range(total):

        @pl.when(scalar_ref[i, 0] == i)
        def _(i=i):
            copy(i).start()

    for done in zero_copies + grad_copies:
        done.wait()
    for i in range(total):

        @pl.when(scalar_ref[i, 0] == i)
        def _(i=i):
            copy(i).wait()


def finish(me, kept, parts, blocks, zeros, residual):
    groups = len(blocks)
    keep = kept.shape[0]
    out_shape = [pltpu.HBM(a.shape, a.dtype) for a in (zeros, residual)]
    out_specs = [hbm(), hbm()]
    scratch = [
        pltpu.VMEM((groups * keep, BLK, BLK), jnp.float32),
        pltpu.VMEM((groups * keep, BLK), jnp.int32),
        pltpu.SMEM((groups * keep, BLK), jnp.int32),
        pltpu.VMEM((BLK, BLK), jnp.bfloat16),
        pltpu.SemaphoreType.DMA((groups * keep,)),
        pltpu.SemaphoreType.DMA,
        pltpu.SemaphoreType.DMA((keep,)),
    ]
    if parts:
        out_shape.insert(0, pltpu.HBM(parts[0].shape, jnp.bfloat16))
        out_specs.insert(0, hbm())
        scratch += [pltpu.VMEM(parts[0].shape, jnp.bfloat16), pltpu.SemaphoreType.DMA((4,))]
        parts = [in_vmem(parts[0]), parts[1]]
    first = 2 + len(parts) + groups
    return pl.pallas_call(
        functools.partial(finish_kernel, groups, keep, bool(parts), residual.shape[1] // BLK),
        out_shape=out_shape,
        in_specs=[smem(), smem()] + [vmem()] * (len(parts) + groups) + [hbm(), hbm()],
        out_specs=out_specs,
        scratch_shapes=scratch,
        input_output_aliases={first: len(out_shape) - 2, first + 1: len(out_shape) - 1},
        compiler_params=params(24),
        cost_estimate=cost(groups * keep * BLK * BLK, groups * keep * BLK * BLK * 8),
        name="finish",
    )(me, kept, *parts, *blocks, in_hbm(zeros), in_hbm(residual))


def swapped(x, axis, mask):
    return lax.ppermute(x, axis, [(i, i ^ mask) for i in range(lax.axis_size(axis))])


def of_all_groups(x):
    return [x] + [swapped(x, "dp", mask) for mask in range(1, lax.axis_size("dp"))]


def body(activations, cotangent, weight, residual, step_size, kept_blocks):
    rows, cols = weight.shape
    groups = lax.axis_size("dp")
    owned_count = (rows // BLK) * (cols // BLK) // groups
    kept = kept_blocks.reshape(-1)
    me = lax.axis_index("dp").astype(jnp.int32).reshape(1)
    here = lax.axis_index("tensor").astype(jnp.int32).reshape(1)
    pair = lax.axis_size("tensor") == 2
    if pair:
        act = swapped(activations, "tensor", 1)
        away, acts_t, own, zeros, kept_cot, kept_res = input_grad_partials(
            here, kept, cotangent, weight, residual[0], owned_count, activations
        )
        parts = [own, swapped(away, "tensor", 1)]
    else:
        act = lax.all_gather(activations, "tensor", axis=0, tiled=True)
        acts_t = None
        own, zeros, kept_cot, kept_res = input_grad_partials(
            here, kept, cotangent, weight, residual[0], owned_count, None
        )
        summed = lax.psum_scatter(own, "tensor", scatter_dimension=0, tiled=True)
        parts = []
    acts_t, blocks = kept_blocks_of(kept, step_size, acts_t, act, kept_cot, kept_res, cols // BLK)
    all_blocks = of_all_groups(blocks)
    rounded = residual_of(here, step_size, acts_t, cotangent, residual[0], pair)
    *grads, owned, residual_out = finish(me, kept, parts, all_blocks, zeros, rounded)
    input_grad = grads[0] if pair else summed.astype(jnp.bfloat16)
    return (input_grad, residual_out[None], owned.reshape(1, 1, 1, owned_count, BLK, BLK))


def solution(mesh):
    in_specs = (
        P(("dp", "tensor"), "fsdp"),
        P("dp", "tensor"),
        P("fsdp", "tensor"),
        P("dp", "fsdp", "tensor"),
        P(),
        P("dp", "fsdp", "tensor", None),
    )
    out_specs = (
        P(("dp", "tensor"), "fsdp"),
        P("dp", "fsdp", "tensor"),
        P("dp", "fsdp", "tensor", None, None, None),
    )
    return jax.shard_map(body, mesh=mesh, in_specs=in_specs, out_specs=out_specs, check_vma=False)
```

profile of v0, /device:TPU:1, one launch (start us, length us, event | category | flops | bytes accessed | tf_op | source)
XLA Modules:
  0.0 64.6 jit_solution(7093413002840760391)
XLA Ops:
  0.6 2.1 %collective-permute-start.1 = (bf16[512,1024]{1,0:T(8,128)(2,1)}, bf16[512,1024]{1,0:T(8,128)(2,1)}, u32[]{:S(2)}, u32[]{:S(2)}) collective-permute-start(bf16[512,1024]{1,0:T(8,128)(2,1)} %refs_0_.1), channel_id=1, source_target_pairs={{0,1},{1,0},{2,3},{3,2},{4,5},{5,4},{6,7},{7,6},{8,9},{9,8},{10,11... | collective-permute-start | bytes 3145736 | tf_op jit(solution)/shard_map/ppermute | solution.py:415
  2.8 0.0 copy-start.4
  2.8 24.7 %input_grad_partials.1 = (bf16[512,1024]{1,0:T(8,128)(2,1)}, bf16[1024,1024]{1,0:T(8,128)(2,1)S(1)}, f32[512,1024]{1,0:T(8,128)S(1)}, f32[128,128,128]{2,1,0:T(8...) custom-call(s32[1]{0:T(128)} %bitcast.2.here_ref, s32[8]{0:T(128)} %bitcast.6, ...), custom_call_target="tpu_custom_call" | custom-call | flops 17179869184 | bytes 41943040 | tf_op jit(solution)/shard_map/input_grad_partials/pallas_call | solution.py:181
  27.5 0.0 copy-start
  27.5 1.3 %copy-done = bf16[8,1024,128]{2,1,0:T(8,128)(2,1)} copy-done((bf16[8,1024,128]{2,1,0:T(8,128)(2,1)}, bf16[8,1024,128]{2,1,0:T(8,128)(2,1)S(1)}, u32[]{:S(2)}) %copy-start) | copy-done | bytes 2097176
  28.8 0.0 copy-start.2
  28.8 1.3 %copy-done.2 = f32[512,1024]{1,0:T(8,128)} copy-done((f32[512,1024]{1,0:T(8,128)}, f32[512,1024]{1,0:T(8,128)S(1)}, u32[]{:S(2)}) %copy-start.2) | copy-done | bytes 2097176
  30.2 0.0 collective-permute-start
  30.8 0.0 collective-permute-done.1.refs_1_
  30.9 0.0 copy-done.4
  30.9 0.0 copy-start.1
  30.9 1.6 %copy-done.1 = bf16[8,1024,128]{2,1,0:T(8,128)(2,1)S(1)} copy-done((bf16[8,1024,128]{2,1,0:T(8,128)(2,1)S(1)}, bf16[8,1024,128]{2,1,0:T(8,128)(2,1)}, u32[]{:S(2)}) %copy-start.1) | copy-done | bytes 2097176
  32.5 2.3 %kept_blocks.1 = (bf16[1024,1024]{1,0:T(8,128)(2,1)S(1)}, bf16[1040,128]{1,0:T(8,128)(2,1)S(1)}) custom-call(s32[8]{0:T(128)S(1)} %bitcast.7, f32[1]{0:T(128)S(6)} %copy.15.step_ref, bf16[1024,1024]{1,0:T(8,128)(2,1)S(1)} %get-tuple-element.16.refs_0_, bf16[512,1024]{1,0:T(8,128)(2,1)} %collective-permute-done.1.refs_1_, ...), custom_call_target="tpu_custom_call", output_to_operand_aliasing={{0}: (2, {})} | custom-call | flops 268435456 | bytes 6291456 | tf_op jit(solution)/shard_map/kept_blocks/pallas_call | solution.py:218
  34.8 2.6 %collective-permute-start.4 = (bf16[1040,128]{1,0:T(8,128)(2,1)S(1)}, bf16[1040,128]{1,0:T(8,128)(2,1)S(1)}, u32[]{:S(2)}, u32[]{:S(2)}) collective-permute-start(bf16[1040,128]{1,0:T(8,128)(2,1)S(1)} %get-tuple-element.19.refs_2_), channel_id=1, source_target_pairs={{0,24},{8,16},{16,8},{24,0},{1,25},{9,17},{17,9},{25,1},{2,26},{10... | collective-permute-start | bytes 798728 | tf_op jit(solution)/shard_map/ppermute | solution.py:415
  37.4 0.0 collective-permute-start.3
  37.4 0.5 collective-permute-start.2
  37.8 0.0 copy-start.3
  37.8 22.8 %residual_out.1.refs_7_ = bf16[1024,8192]{1,0:T(8,128)(2,1)} custom-call(s32[1]{0:T(128)} %bitcast.2.here_ref, f32[1]{0:T(128)S(6)} %copy.15.step_ref, bf16[1024,1024]{1,0:T(8,128)(2,1)S(1)} %get-tuple-element.21.acts_t_ref, bf16[1024,8192]{1,0:T(8,128)(2,1)} %cot_ref.3, bf16[1024,8192]{1,0:T(8,128)(2,1)} %bitcast.12), custom_call_target="tpu_custom_call" | custom-call | flops 17179869184 | bytes 52428800 | tf_op jit(solution)/shard_map/residual_out/pallas_call | solution.py:280
  60.6 0.0 collective-permute-done.refs_1_
  60.6 0.0 collective-permute-done.4.refs_5_
  60.6 0.0 collective-permute-done.3.refs_4_
  60.6 0.0 collective-permute-done.2.refs_3_
  60.6 0.0 copy-done.3
  60.7 3.8 %finish.1 = (bf16[512,1024]{1,0:T(8,128)(2,1)}, f32[128,128,128]{2,1,0:T(8,128)}, bf16[1024,8192]{1,0:T(8,128)(2,1)}) custom-call(s32[1]{0:T(128)} %bitcast.me_ref, s32[8]{0:T(128)S(1)} %bitcast.8, f32[512,1024]{1,0:T(8,128)S(1)} %copy-done.3, bf16[512,1024]{1,0:T(8,128)(2,1)S(1)} %collective-permute-done.refs_1_, ...), custom_call_target="tpu_custom_call", output_to_operand_aliasing={{1}: (8, {}), {2}: (9, {})} | custom-call | flops 524288 | bytes 4194304 | tf_op jit(solution)/shard_map/finish/pallas_call | solution.py:401
Async XLA Ops:
  0.6 30.2 %collective-permute-start.1 = (bf16[512,1024]{1,0:T(8,128)(2,1)}, bf16[512,1024]{1,0:T(8,128)(2,1)}, u32[]{:S(2)}, u32[]{:S(2)}) collective-permute-start(bf16[512,1024]{1,0:T(8,128)(2,1)} %refs_0_.1), channel_id=1, source_target_pairs={{0,1},{1,0},{2,3},{3,2},{4,5},{5,4},{6,7},{7,6},{8,9},{9,8},{10,11... | collective-permute-start | bytes 3145736 | tf_op jit(solution)/shard_map/ppermute | solution.py:415
  2.8 28.1 %copy-start.4 = (s32[1,1,1,8]{3,2,1,0:T(1,128)S(1)}, s32[1,1,1,8]{3,2,1,0:T(1,128)}, u32[]{:S(2)}) copy-start(s32[1,1,1,8]{3,2,1,0:T(1,128)} %param.11) | copy-start | bytes 100
  27.5 1.3 %copy-start = (bf16[8,1024,128]{2,1,0:T(8,128)(2,1)}, bf16[8,1024,128]{2,1,0:T(8,128)(2,1)S(1)}, u32[]{:S(2)}) copy-start(bf16[8,1024,128]{2,1,0:T(8,128)(2,1)S(1)} %get-tuple-element.17.refs_2_) | copy-start | bytes 6291460
  28.8 1.3 %copy-start.2 = (f32[512,1024]{1,0:T(8,128)}, f32[512,1024]{1,0:T(8,128)S(1)}, u32[]{:S(2)}) copy-start(f32[512,1024]{1,0:T(8,128)S(1)} %get-tuple-element.14.refs_0_) | copy-start | bytes 6291460
  30.2 30.4 %collective-permute-start = (bf16[512,1024]{1,0:T(8,128)(2,1)}, bf16[512,1024]{1,0:T(8,128)(2,1)S(1)}, u32[]{:S(2)}, u32[]{:S(2)}) collective-permute-start(bf16[512,1024]{1,0:T(8,128)(2,1)} %get-tuple-element.15), channel_id=1, source_target_pairs={{0,1},{1,0},{2,3},{3,2},{4,5},{5,4},{6,7},{7,6},{8,9},{9,8},{10,11... | collective-permute-start | bytes 3145736 | tf_op jit(solution)/shard_map/ppermute | solution.py:415
  30.9 1.6 %copy-start.1 = (bf16[8,1024,128]{2,1,0:T(8,128)(2,1)S(1)}, bf16[8,1024,128]{2,1,0:T(8,128)(2,1)}, u32[]{:S(2)}) copy-start(bf16[8,1024,128]{2,1,0:T(8,128)(2,1)} %copy-done) | copy-start | bytes 6291460
  34.8 25.9 %collective-permute-start.4 = (bf16[1040,128]{1,0:T(8,128)(2,1)S(1)}, bf16[1040,128]{1,0:T(8,128)(2,1)S(1)}, u32[]{:S(2)}, u32[]{:S(2)}) collective-permute-start(bf16[1040,128]{1,0:T(8,128)(2,1)S(1)} %get-tuple-element.19.refs_2_), channel_id=1, source_target_pairs={{0,24},{8,16},{16,8},{24,0},{1,25},{9,17},{17,9},{25,1},{2,26},{10... | collective-permute-start | bytes 798728 | tf_op jit(solution)/shard_map/ppermute | solution.py:415
  37.4 23.3 %collective-permute-start.3 = (bf16[1040,128]{1,0:T(8,128)(2,1)S(1)}, bf16[1040,128]{1,0:T(8,128)(2,1)S(1)}, u32[]{:S(2)}, u32[]{:S(2)}) collective-permute-start(bf16[1040,128]{1,0:T(8,128)(2,1)S(1)} %get-tuple-element.19.refs_2_), channel_id=1, source_target_pairs={{0,16},{8,24},{16,0},{24,8},{1,17},{9,25},{17,1},{25,9},{2,18},{10... | collective-permute-start | bytes 798728 | tf_op jit(solution)/shard_map/ppermute | solution.py:415
  37.4 23.3 %collective-permute-start.2 = (bf16[1040,128]{1,0:T(8,128)(2,1)S(1)}, bf16[1040,128]{1,0:T(8,128)(2,1)S(1)}, u32[]{:S(2)}, u32[]{:S(2)}) collective-permute-start(bf16[1040,128]{1,0:T(8,128)(2,1)S(1)} %get-tuple-element.19.refs_2_), channel_id=1, source_target_pairs={{0,8},{8,0},{16,24},{24,16},{1,9},{9,1},{17,25},{25,17},{2,10},{10... | collective-permute-start | bytes 798728 | tf_op jit(solution)/shard_map/ppermute | solution.py:415
  37.8 22.8 %copy-start.3 = (f32[512,1024]{1,0:T(8,128)S(1)}, f32[512,1024]{1,0:T(8,128)}, u32[]{:S(2)}) copy-start(f32[512,1024]{1,0:T(8,128)} %copy-done.2) | copy-start | bytes 6291460
where the time goes:
time: 64.4 us; the launch traced here: 64.6 us
  Pallas kernels  53.6 us (83%)
  starting transfers between devices  5.23 us (8%)
  local copies, waits for them, and re-layouts  4.24 us (7%)
  between operations  1.54 us (2%)
    pallas_call x1, Pallas kernels, input_grad_partials(): pl.pallas_call(functools.partial(input_grad_kernel, split, sizes, zero_co...  24.7 us
    pallas_call x1, Pallas kernels, residual_of(): pl.pallas_call(functools.partial(residual_kernel, split), out_shape=pltpu...  22.8 us
    ppermute x5, starting transfers between devices, swapped(): lax.ppermute(x, axis, [(i, i ^ mask) for i in range(lax.axis_size(axis))])  5.23 us
    unnamed x10, local copies, waits for them, and re-layouts  4.24 us
    pallas_call x1, Pallas kernels, finish(): pl.pallas_call(functools.partial(finish_kernel, groups, keep, bool(parts)...  3.76 us
    pallas_call x1, Pallas kernels, kept_blocks_of(): pl.pallas_call(functools.partial(kept_kernel, pair, col_blocks), out_shap...  2.3 us
  transfers between devices with their start and end apart: 5, of which 0 were waited for; matrix products, arithmetic and copies ran while one was open for 0% of the time, Pallas kernels for 77%

commit v1 on v0

--- a/solution.py
+++ b/solution.py
@@ -31,11 +31,11 @@
 
 def hidden_chunks(cols):
     sizes = []
-    for size in (512, 1536, 2048, 4096):
+    for size in (512, 1024, 2048, 4608):
         if cols > sum(sizes):
             sizes.append(min(size, cols - sum(sizes)))
     while sum(sizes) < cols:
-        sizes.append(min(4096, cols - sum(sizes)))
+        sizes.append(min(4608, cols - sum(sizes)))
     return sizes
 
 
@@ -70,16 +70,16 @@
     return copies
 
 
-def input_grad_kernel(split, sizes, zero_copies, here_ref, kept_ref, cot_ref, w_ref, res_ref, *refs):
+def input_grad_kernel(split, sizes, zero_copies, here_ref, _, kept_ref, cot_ref, w_ref, res_ref, *refs):
     if split:
         acts_ref, away_ref, acts_t_ref, *refs = refs
-    own_ref, owned_ref, kept_cot_ref, kept_res_ref, *refs = refs
-    acc_ref, cot_buf, w_buf, zero_ref, cot_sem, w_sem, zero_sem, kept_cot_sem, kept_res_sem, *refs = refs
+    own_ref, owned_ref, cot_buf, kept_res_ref, *refs = refs
+    acc_ref, w_buf, zero_ref, cot_sem, w_sem, zero_sem, kept_res_sem, *refs = refs
     zero_rows = zero_ref.shape[0]
     rows, hidden = w_ref.shape
     width = min(256, rows)
     last = len(sizes) - 1
-    keep = kept_cot_ref.shape[0]
+    keep = kept_res_ref.shape[0]
     half = own_ref.shape[0]
 
     def loads(i):
@@ -96,39 +96,37 @@
     def zero_copy(i):
         return pltpu.make_async_copy(zero_ref, owned_ref.at[pl.ds(i * zero_rows, zero_rows)], zero_sem.at[i])
 
-    def kept_copies(k):
+    def kept_copy(k):
         col_blocks = hidden // BLK
         row = pl.ds(pl.multiple_of(kept_ref[k] // col_blocks * BLK, BLK), BLK)
         col = pl.ds(pl.multiple_of(kept_ref[k] % col_blocks * BLK, BLK), BLK)
-        return (
-            pltpu.make_async_copy(cot_buf.at[:, col], kept_cot_ref.at[k], kept_cot_sem.at[k]),
-            pltpu.make_async_copy(res_ref.at[row, col], kept_res_ref.at[k], kept_res_sem.at[k]),
-        )
-
+        return pltpu.make_async_copy(res_ref.at[row, col], kept_res_ref.at[k], kept_res_sem.at[k])
+
+    start(0)
+    start(1)
     if split:
         acts_buf, acts_sem = refs
         acts_copy = pltpu.make_async_copy(acts_ref, acts_buf, acts_sem)
         acts_copy.start()
-    start(0)
-    if split:
-        acts_copy.wait()
-        acts_t_ref[:, :half] = acts_buf[...].T
-    start(1)
     zero_ref[...] = jnp.zeros_like(zero_ref)
+    turned = min(1, last)
     for i in range(last + 1):
         for copy in loads(i):
             copy.wait()
+        if split and i == turned:
+            acts_copy.wait()
         start(i + 2)
         if i == last:
             for z in range(zero_copies):
                 zero_copy(z).start()
             for k in range(keep):
-                for copy in kept_copies(k):
-                    copy.start()
+                kept_copy(k).start()
         part = slice(sum(sizes[:i]), sum(sizes[: i + 1]))
         for at in range(0, rows, width):
             cols = slice(at, at + width)
             total = dot_nt(cot_buf[:, part], w_buf[cols, part])
+            if split and i == turned:
+                acts_t_ref[cols, :half] = acts_buf[:, cols].T
             if i > 0:
                 total += acc_ref[:, cols]
             if i < last:
@@ -140,11 +138,10 @@
     for z in range(zero_copies):
         zero_copy(z).wait()
     for k in range(keep):
-        for copy in kept_copies(k):
-            copy.wait()
-
-
-def input_grad_partials(here, kept, cot, weight, residual, owned_count, acts):
+        kept_copy(k).wait()
+
+
+def input_grad_partials(here, me, kept, cot, weight, residual, owned_count, acts):
     split = acts is not None
     tokens, cols = cot.shape
     rows = weight.shape[0]
@@ -156,19 +153,17 @@
     out_shape = [
         pltpu.VMEM((own_rows, rows), jnp.float32) if split else jax.ShapeDtypeStruct((own_rows, rows), jnp.float32),
         pltpu.HBM((owned_count, BLK, BLK), jnp.float32),
-        pltpu.VMEM((keep, tokens, BLK), jnp.bfloat16),
+        pltpu.VMEM((tokens, cols), jnp.bfloat16),
         pltpu.VMEM((keep, BLK, BLK), jnp.bfloat16),
     ]
     out_specs = [vmem(), hbm(), vmem(), vmem()]
     scratch = [
         pltpu.VMEM((tokens, rows), jnp.float32),
-        pltpu.VMEM((tokens, cols), jnp.bfloat16),
         pltpu.VMEM((rows, cols), jnp.bfloat16),
         pltpu.VMEM((zero_rows, BLK, BLK), jnp.float32),
         pltpu.SemaphoreType.DMA((len(sizes), 2)),
         pltpu.SemaphoreType.DMA((len(sizes),)),
         pltpu.SemaphoreType.DMA((zero_copies,)),
-        pltpu.SemaphoreType.DMA((keep,)),
         pltpu.SemaphoreType.DMA((keep,)),
     ]
     if split:
@@ -181,25 +176,31 @@
     return pl.pallas_call(
         functools.partial(input_grad_kernel, split, sizes, zero_copies),
         out_shape=out_shape,
-        in_specs=[smem(), smem()] + [hbm()] * (3 + split),
+        in_specs=[smem()] * 3 + [hbm()] * (3 + split),
         out_specs=out_specs,
         scratch_shapes=scratch,
-        compiler_params=params(52),
+        compiler_params=params(34),
         cost_estimate=cost(2 * tokens * rows * cols, 2 * cols * (tokens + rows) + 4 * owned_count * BLK * BLK),
         name="input_grad_partials",
-    )(here, kept, in_hbm(cot), in_hbm(weight), in_hbm(residual), *([in_hbm(acts)] if split else []))
-
-
-def kept_kernel(pair, col_blocks, kept_ref, step_ref, *refs):
+    )(here, me, kept, in_hbm(cot), in_hbm(weight), in_hbm(residual), *([in_hbm(acts)] if split else []))
+
+
+def kept_kernel(pair, kept_ref, step_in, *refs):
     if pair:
         _, *refs = refs
-    act_ref, cot_ref, res_ref, acts_t_ref, out_ref = refs
-    keep = cot_ref.shape[0]
+    act_ref, cot_ref, kept_res_ref, acts_t_ref, out_ref, step_ref, step_sem = refs
+    keep = kept_res_ref.shape[0]
+    col_blocks = cot_ref.shape[1] // BLK
+    step_copy = pltpu.make_async_copy(step_in, step_ref, step_sem)
+    step_copy.start()
     acts_t_ref[:, acts_t_ref.shape[1] - act_ref.shape[0] :] = act_ref[...].T
+    step_copy.wait()
+    step = step_ref[0]
     for k in range(keep):
         row = pl.ds(pl.multiple_of(kept_ref[k] // col_blocks * BLK, BLK), BLK)
-        gradient = dot_nn(acts_t_ref[row, :], cot_ref[k])
-        out_ref[k * BLK : (k + 1) * BLK, :] = (res_ref[k].astype(jnp.float32) + step_ref[0] * gradient).astype(
+        col = pl.ds(pl.multiple_of(kept_ref[k] % col_blocks * BLK, BLK), BLK)
+        gradient = dot_nn(acts_t_ref[row, :], cot_ref[:, col])
+        out_ref[k * BLK : (k + 1) * BLK, :] = (kept_res_ref[k].astype(jnp.float32) + step * gradient).astype(
             jnp.bfloat16
         )
     lane = lax.broadcasted_iota(jnp.int32, (LABEL_ROWS, BLK), 1) % keep
@@ -211,88 +212,99 @@
     out_ref[keep * BLK :, :] = label.astype(jnp.float32).astype(jnp.bfloat16)
 
 
-def kept_blocks_of(kept, step_size, acts_t, act, kept_cot, kept_res, col_blocks):
+def kept_blocks_of(kept, step_size, acts_t, act, cot, kept_res):
     rows = act.shape[1]
-    keep, tokens = kept_cot.shape[:2]
+    tokens, cols = cot.shape
+    keep = kept_res.shape[0]
     pair = acts_t is not None
     return pl.pallas_call(
-        functools.partial(kept_kernel, pair, col_blocks),
+        functools.partial(kept_kernel, pair),
         out_shape=[
             pltpu.VMEM((rows, tokens), jnp.bfloat16),
             jax.ShapeDtypeStruct((keep * BLK + LABEL_ROWS, BLK), jnp.bfloat16),
         ],
-        in_specs=[smem()] * 2 + [vmem()] * (3 + pair),
-        out_specs=[vmem(), vmem()],
+        in_specs=[smem(), pl.BlockSpec(memory_space=pl.ANY)] + [vmem()] * (3 + pair),
+        out_specs=[vmem()] * 2,
+        scratch_shapes=[pltpu.SMEM((1,), jnp.float32), pltpu.SemaphoreType.DMA],
         input_output_aliases={2: 0} if pair else {},
-        compiler_params=params(16),
+        compiler_params=params(4),
         cost_estimate=cost(2 * tokens * BLK * BLK * keep, 4 * tokens * rows + 2 * keep * tokens * BLK),
         name="kept_blocks",
-    )(kept, step_size, *([in_vmem(acts_t)] if pair else []), act, in_vmem(kept_cot), in_vmem(kept_res))
-
-
-def residual_kernel(split, here_ref, step_ref, acts_t_ref, cot_ref, res_ref, out_ref, cot_buf, res_buf, *sems):
-    cot_sem, res_sem, out_sem = sems
-    step = step_ref[0]
-    chunks, _, chunk = cot_buf.shape
+    )(
+        kept,
+        step_size,
+        *([in_vmem(acts_t)] if pair else []),
+        act,
+        in_vmem(cot),
+        in_vmem(kept_res),
+    )
+
+
+def residual_kernel(step_in, acts_t_ref, cot_ref, res_ref, out_ref, res_buf, step_ref, step_sem, res_sem, out_sem):
+    chunks, _, chunk = res_buf.shape
     width = min(256, chunk)
-
-    def columns(j):
-        return pl.ds(pl.multiple_of(j * chunk, chunk), chunk)
-
-    def loads(j):
-        return cot_copies(here_ref, split, cot_ref.at[:, columns(j)], cot_buf.at[j], cot_sem.at[j]) + [
-            pltpu.make_async_copy(res_ref.at[:, columns(j)], res_buf.at[j], res_sem.at[j])
-        ]
-
-    def store(j):
-        return pltpu.make_async_copy(res_buf.at[j], out_ref.at[:, columns(j)], out_sem.at[j])
+    pieces = chunk // width
+
+    def load(j):
+        cols = pl.ds(pl.multiple_of(j * chunk, chunk), chunk)
+        return pltpu.make_async_copy(res_ref.at[:, cols], res_buf.at[j], res_sem.at[j])
+
+    def store(j, n):
+        cols = pl.ds(pl.multiple_of(j * chunk + n * width, width), width)
+        return pltpu.make_async_copy(
+            res_buf.at[j, :, pl.ds(n * width, width)], out_ref.at[:, cols], out_sem.at[j, n]
+        )
 
     def start(j):
         @pl.when(j < chunks)
         def _():
-            for copy in loads(j):
-                copy.start()
-
+            load(j).start()
+
+    step_copy = pltpu.make_async_copy(step_in, step_ref, step_sem)
+    step_copy.start()
     start(0)
     start(1)
+    step_copy.wait()
+    step = step_ref[0]
 
     @pl.loop(0, chunks)
     def _(j):
-        for copy in loads(j):
-            copy.wait()
+        load(j).wait()
         start(j + 2)
-        for at in range(0, chunk, width):
-            part = slice(at, at + width)
-            gradient = dot_nn(acts_t_ref[...], cot_buf[j, :, part])
+        for n in range(pieces):
+            part = slice(n * width, (n + 1) * width)
+            cols = pl.ds(pl.multiple_of(j * chunk + n * width, width), width)
+            gradient = dot_nn(acts_t_ref[...], cot_ref[:, cols])
             res_buf[j, :, part] = (res_buf[j, :, part].astype(jnp.float32) + step * gradient).astype(jnp.bfloat16)
-        store(j).start()
-
-    for j in range(chunks):
-        store(j).wait()
-
-
-def residual_of(here, step_size, acts_t, cot, residual, split):
+            store(j, n).start()
+
+    @pl.loop(0, chunks)
+    def _(j):
+        for n in range(pieces):
+            store(j, n).wait()
+
+
+def residual_of(step_size, acts_t, cot, residual):
     tokens, cols = cot.shape
     rows = residual.shape[0]
     chunk = min(1024, cols)
     chunks = cols // chunk
-    sem = pltpu.SemaphoreType.DMA((chunks,))
     return pl.pallas_call(
-        functools.partial(residual_kernel, split),
+        residual_kernel,
         out_shape=pltpu.HBM((rows, cols), jnp.bfloat16),
-        in_specs=[smem()] * 2 + [vmem(), hbm(), hbm()],
+        in_specs=[pl.BlockSpec(memory_space=pl.ANY), vmem(), vmem(), hbm()],
         out_specs=hbm(),
         scratch_shapes=[
-            pltpu.VMEM((chunks, tokens, chunk), jnp.bfloat16),
             pltpu.VMEM((chunks, rows, chunk), jnp.bfloat16),
-            pltpu.SemaphoreType.DMA((chunks, 2)),
-            sem,
-            sem,
+            pltpu.SMEM((1,), jnp.float32),
+            pltpu.SemaphoreType.DMA,
+            pltpu.SemaphoreType.DMA((chunks,)),
+            pltpu.SemaphoreType.DMA((chunks, chunk // min(256, chunk))),
         ],
-        compiler_params=params(44),
-        cost_estimate=cost(2 * tokens * rows * cols, 2 * tokens * (rows + cols) + 4 * rows * cols),
+        compiler_params=params(20),
+        cost_estimate=cost(2 * tokens * rows * cols, 2 * tokens * rows + 4 * rows * cols),
         name="residual_out",
-    )(here, step_size, in_vmem(acts_t), in_hbm(cot), in_hbm(residual))
+    )(step_size, in_vmem(acts_t), in_vmem(cot), in_hbm(residual))
 
 
 def finish_kernel(groups, keep, pair, col_blocks, me_ref, kept_ref, *refs):
@@ -405,7 +417,7 @@
         out_specs=out_specs,
         scratch_shapes=scratch,
         input_output_aliases={first: len(out_shape) - 2, first + 1: len(out_shape) - 1},
-        compiler_params=params(24),
+        compiler_params=params(10),
         cost_estimate=cost(groups * keep * BLK * BLK, groups * keep * BLK * BLK * 8),
         name="finish",
     )(me, kept, *parts, *blocks, in_hbm(zeros), in_hbm(residual))
@@ -429,21 +441,21 @@
     pair = lax.axis_size("tensor") == 2
     if pair:
         act = swapped(activations, "tensor", 1)
-        away, acts_t, own, zeros, kept_cot, kept_res = input_grad_partials(
-            here, kept, cotangent, weight, residual[0], owned_count, activations
+        away, acts_t, own, zeros, cot, kept_res = input_grad_partials(
+            here, me, kept, cotangent, weight, residual[0], owned_count, activations
         )
         parts = [own, swapped(away, "tensor", 1)]
     else:
         act = lax.all_gather(activations, "tensor", axis=0, tiled=True)
         acts_t = None
-        own, zeros, kept_cot, kept_res = input_grad_partials(
-            here, kept, cotangent, weight, residual[0], owned_count, None
+        own, zeros, cot, kept_res = input_grad_partials(
+            here, me, kept, cotangent, weight, residual[0], owned_count, None
         )
         summed = lax.psum_scatter(own, "tensor", scatter_dimension=0, tiled=True)
         parts = []
-    acts_t, blocks = kept_blocks_of(kept, step_size, acts_t, act, kept_cot, kept_res, cols // BLK)
+    acts_t, blocks = kept_blocks_of(kept, step_size, acts_t, act, cot, kept_res)
     all_blocks = of_all_groups(blocks)
-    rounded = residual_of(here, step_size, acts_t, cotangent, residual[0], pair)
+    rounded = residual_of(step_size, acts_t, cot, residual[0])
     *grads, owned, residual_out = finish(me, kept, parts, all_blocks, zeros, rounded)
     input_grad = grads[0] if pair else summed.astype(jnp.bfloat16)
     return (input_grad, residual_out[None], owned.reshape(1, 1, 1, owned_count, BLK, BLK))

time: 64.4 us -> 61.3 us (0.952); the launches traced: 64.6 us -> 60.5 us
  local copies, waits for them, and re-layouts: 4.24 us -> 0.01 us
    unnamed x10 -> x2, local copies, waits for them, and re-layouts: 4.24 us -> 0.01 us
    pallas_call x1, Pallas kernels: 24.7 us -> 25.9 us  [input_grad_partials(): pl.pallas_call(functools.partial(input_grad_kernel, split, sizes, zero_co...]
    pallas_call x1, Pallas kernels: 3.76 us -> 2.7 us  [finish(): pl.pallas_call(functools.partial(finish_kernel, groups, keep, bool(parts)...]
  transfers between devices with their start and end apart: 5 -> 5, of which waited for: 0 -> 0; matrix products, arithmetic and copies ran while one was open for 0% -> 0% of each run, Pallas kernels for 77% -> 84%
where the time goes in v1:
time: 61.3 us; the launch traced here: 60.5 us
  Pallas kernels  53.7 us (88%)
  starting transfers between devices  5.29 us (9%)
  between operations  1.52 us (2%)
    pallas_call x1, Pallas kernels, input_grad_partials(): pl.pallas_call(functools.partial(input_grad_kernel, split, sizes, zero_co...  25.9 us
    pallas_call x1, Pallas kernels, residual_of(): pl.pallas_call(residual_kernel, out_shape=pltpu.HBM((rows, cols), jnp.bfl...  23.1 us
    ppermute x5, starting transfers between devices, swapped(): lax.ppermute(x, axis, [(i, i ^ mask) for i in range(lax.axis_size(axis))])  5.29 us
    pallas_call x1, Pallas kernels, finish(): pl.pallas_call(functools.partial(finish_kernel, groups, keep, bool(parts)...  2.7 us
    pallas_call x1, Pallas kernels, kept_blocks_of(): pl.pallas_call(functools.partial(kept_kernel, pair), out_shape=[pltpu.VME...  1.98 us
  transfers between devices with their start and end apart: 5, of which 0 were waited for; matrix products, arithmetic and copies ran while one was open for 0% of the time, Pallas kernels for 84%

profile of v1, /device:TPU:1, one launch (start us, length us, event | category | flops | bytes accessed | tf_op | source)
XLA Modules:
  0.0 60.5 jit_solution(12720696261303878407)
XLA Ops:
  0.6 2.1 %collective-permute-start.1 = (bf16[512,1024]{1,0:T(8,128)(2,1)}, bf16[512,1024]{1,0:T(8,128)(2,1)S(1)}, u32[]{:S(2)}, u32[]{:S(2)}) collective-permute-start(bf16[512,1024]{1,0:T(8,128)(2,1)} %refs_0_.1), channel_id=1, source_target_pairs={{0,1},{1,0},{2,3},{3,2},{4,5},{5,4},{6,7},{7,6},{8,9},{9,8},{10,11... | collective-permute-start | bytes 3145736 | tf_op jit(solution)/shard_map/ppermute | solution.py:427
  2.8 0.0 copy-start
  2.8 25.9 %input_grad_partials.1 = (bf16[512,1024]{1,0:T(8,128)(2,1)}, bf16[1024,1024]{1,0:T(8,128)(2,1)S(1)}, f32[512,1024]{1,0:T(8,128)S(1)}, f32[128,128,128]{2,1,0:T(8...) custom-call(s32[1]{0:T(128)} %bitcast.2.here_ref, s32[1]{0:T(128)} %bitcast._.me_ref, s32[8]{0:T(128)} %bitcast.6, ...), custom_call_target="tpu_custom_call" | custom-call | flops 17179869184 | bytes 41943040 | tf_op jit(solution)/shard_map/input_grad_partials/pallas_call | solution.py:176
  28.7 0.1 collective-permute-start
  29.4 0.0 collective-permute-done.1.refs_1_
  29.4 0.0 copy-done
  29.4 2.0 %kept_blocks.1 = (bf16[1024,1024]{1,0:T(8,128)(2,1)S(1)}, bf16[1040,128]{1,0:T(8,128)(2,1)S(1)}) custom-call(s32[8]{0:T(128)S(1)} %bitcast.7, f32[1]{0:T(128)S(6)} %copy.15.step_in, bf16[1024,1024]{1,0:T(8,128)(2,1)S(1)} %get-tuple-element.16.refs_0_, bf16[512,1024]{1,0:T(8,128)(2,1)S(1)} %collective-permute-done.1.refs_1_, ...), custom_call_target="tpu_custom_call", output_to_operand_aliasing={{0}: (2, {})} | custom-call | flops 268435456 | bytes 6291456 | tf_op jit(solution)/shard_map/kept_blocks/pallas_call | solution.py:220
  31.4 2.6 %collective-permute-start.4 = (bf16[1040,128]{1,0:T(8,128)(2,1)S(1)}, bf16[1040,128]{1,0:T(8,128)(2,1)S(1)}, u32[]{:S(2)}, u32[]{:S(2)}) collective-permute-start(bf16[1040,128]{1,0:T(8,128)(2,1)S(1)} %get-tuple-element.19.refs_2_), channel_id=1, source_target_pairs={{0,24},{8,16},{16,8},{24,0},{1,25},{9,17},{17,9},{25,1},{2,26},{10... | collective-permute-start | bytes 798728 | tf_op jit(solution)/shard_map/ppermute | solution.py:427
  34.0 0.0 collective-permute-start.3
  34.0 0.5 collective-permute-start.2
  34.5 23.1 %residual_out.1.refs_7_ = bf16[1024,8192]{1,0:T(8,128)(2,1)} custom-call(f32[1]{0:T(128)S(6)} %copy.15.step_in, bf16[1024,1024]{1,0:T(8,128)(2,1)S(1)} %get-tuple-element.21.acts_t_ref, bf16[1024,8192]{1,0:T(8,128)(2,1)S(1)} %get-tuple-element.17.refs_2_.cot_ref, bf16[1024,8192]{1,0:T(8,128)(2,1)} %bitcast.12), custom_call_target="tpu_custom_call" | custom-call | flops 17179869184 | bytes 35651584 | tf_op jit(solution)/shard_map/residual_out/pallas_call | solution.py:292
  57.6 0.0 collective-permute-done.refs_1_
  57.6 0.0 collective-permute-done.4.refs_5_
  57.6 0.0 collective-permute-done.3.refs_4_
  57.6 0.0 collective-permute-done.2.refs_3_
  57.7 2.7 %finish.1 = (bf16[512,1024]{1,0:T(8,128)(2,1)}, f32[128,128,128]{2,1,0:T(8,128)}, bf16[1024,8192]{1,0:T(8,128)(2,1)}) custom-call(s32[1]{0:T(128)} %bitcast._.me_ref, s32[8]{0:T(128)S(1)} %bitcast.8, f32[512,1024]{1,0:T(8,128)S(1)} %get-tuple-element.14.refs_0_, ...), custom_call_target="tpu_custom_call", output_to_operand_aliasing={{1}: (8, {}), {2}: (9, {})} | custom-call | flops 524288 | bytes 4194304 | tf_op jit(solution)/shard_map/finish/pallas_call | solution.py:413
Async XLA Ops:
  0.6 28.8 %collective-permute-start.1 = (bf16[512,1024]{1,0:T(8,128)(2,1)}, bf16[512,1024]{1,0:T(8,128)(2,1)S(1)}, u32[]{:S(2)}, u32[]{:S(2)}) collective-permute-start(bf16[512,1024]{1,0:T(8,128)(2,1)} %refs_0_.1), channel_id=1, source_target_pairs={{0,1},{1,0},{2,3},{3,2},{4,5},{5,4},{6,7},{7,6},{8,9},{9,8},{10,11... | collective-permute-start | bytes 3145736 | tf_op jit(solution)/shard_map/ppermute | solution.py:427
  2.8 26.7 %copy-start = (s32[1,1,1,8]{3,2,1,0:T(1,128)S(1)}, s32[1,1,1,8]{3,2,1,0:T(1,128)}, u32[]{:S(2)}) copy-start(s32[1,1,1,8]{3,2,1,0:T(1,128)} %param.11) | copy-start | bytes 100
  28.7 28.9 %collective-permute-start = (bf16[512,1024]{1,0:T(8,128)(2,1)}, bf16[512,1024]{1,0:T(8,128)(2,1)S(1)}, u32[]{:S(2)}, u32[]{:S(2)}) collective-permute-start(bf16[512,1024]{1,0:T(8,128)(2,1)} %get-tuple-element.15), channel_id=1, source_target_pairs={{0,1},{1,0},{2,3},{3,2},{4,5},{5,4},{6,7},{7,6},{8,9},{9,8},{10,11... | collective-permute-start | bytes 3145736 | tf_op jit(solution)/shard_map/ppermute | solution.py:427
  31.4 26.2 %collective-permute-start.4 = (bf16[1040,128]{1,0:T(8,128)(2,1)S(1)}, bf16[1040,128]{1,0:T(8,128)(2,1)S(1)}, u32[]{:S(2)}, u32[]{:S(2)}) collective-permute-start(bf16[1040,128]{1,0:T(8,128)(2,1)S(1)} %get-tuple-element.19.refs_2_), channel_id=1, source_target_pairs={{0,24},{8,16},{16,8},{24,0},{1,25},{9,17},{17,9},{25,1},{2,26},{10... | collective-permute-start | bytes 798728 | tf_op jit(solution)/shard_map/ppermute | solution.py:427
  34.0 23.6 %collective-permute-start.3 = (bf16[1040,128]{1,0:T(8,128)(2,1)S(1)}, bf16[1040,128]{1,0:T(8,128)(2,1)S(1)}, u32[]{:S(2)}, u32[]{:S(2)}) collective-permute-start(bf16[1040,128]{1,0:T(8,128)(2,1)S(1)} %get-tuple-element.19.refs_2_), channel_id=1, source_target_pairs={{0,16},{8,24},{16,0},{24,8},{1,17},{9,25},{17,1},{25,9},{2,18},{10... | collective-permute-start | bytes 798728 | tf_op jit(solution)/shard_map/ppermute | solution.py:427
  34.0 23.6 %collective-permute-start.2 = (bf16[1040,128]{1,0:T(8,128)(2,1)S(1)}, bf16[1040,128]{1,0:T(8,128)(2,1)S(1)}, u32[]{:S(2)}, u32[]{:S(2)}) collective-permute-start(bf16[1040,128]{1,0:T(8,128)(2,1)S(1)} %get-tuple-element.19.refs_2_), channel_id=1, source_target_pairs={{0,8},{8,0},{16,24},{24,16},{1,9},{9,1},{17,25},{25,17},{2,10},{10... | collective-permute-start | bytes 798728 | tf_op jit(solution)/shard_map/ppermute | solution.py:427
